TPU v7x, 32 devices: a whole 2x2x4 slice. The times are simulated.
32 devices in a mesh: seq: 8 (over z, x), head: 4 (over y, core).
Axes of the slice: x: 2, y: 2, z: 4, core: 2. Of those that a mesh axis runs over, the one named last changes fastest.
Arguments:
- queries: bfloat16 [8192, 4096], P(('seq', 'head')), may hold values from -5 to 5
- keys: bfloat16 [8192, 1024], P(('seq', 'head')), may hold values from -5 to 5
- values: bfloat16 [8192, 1024], P(('seq', 'head')), may hold values from -6 to 6
- upstream: bfloat16 [8192, 4096], P('seq', 'head'), may hold values from -6 to 6
- lengths: int32 [8, 8], P('seq'), may hold values from 1 to 122, as said below
- guests: int32 [8, 8], P('seq'), may hold values from 0 to 1, as said below
- advantage: float32 [8, 8], P('seq'), may hold values from -4 to 4
- partner: int32 [8], replicated, may hold values from 0 to 7, as said below
Outputs:
- grad_q: bfloat16 [8192, 4096], P(('seq', 'head'))
- grad_k: bfloat16 [8192, 1024], P(('seq', 'head'))
- grad_v: bfloat16 [8192, 1024], P(('seq', 'head'))
Inputs may be any that keep to these rules, and one draw needn't show every extreme that they name: `lengths`: every tree has a slot with a response of 122 tokens; rows of a slot beyond its length are padding. `guests`: every tree has at least one guest slot. The pairing is mutual and never pairs a tree with itself: partner[partner[i]] = i.
All inputs are finite; a program needn't handle non-finite values.
Results may differ from a plain program's by a relative error of at most 0.025.
Values may be sent and summed in bfloat16 or wider, within the bound.
A program may use at most 64 MiB of HBM per device.

v0:
```python
import functools
import math

import jax
import jax.numpy as jnp
from jax import lax
from jax.experimental import pallas as pl
from jax.experimental.pallas import tpu as pltpu
from jax.sharding import PartitionSpec as P

HEAD_DIM = 128
PROMPT = 48
RESP_LEN = 122
TILE = 128
PAD = 128
HALO = 128
LOGICAL = pl.DeviceIdType.MESH
BF16 = jnp.bfloat16
F32 = jnp.float32


def mix(a, b, size):
    out = 0
    bit = 1
    while bit < size:
        out = out + lax.rem(lax.div(a, bit) + lax.div(b, bit), 2) * bit
        bit *= 2
    return out


def dot(a, b, da, db):
    return lax.dot_general(a, b, (((da,), (db,)), ((), ())), preferred_element_type=F32)


def kernel(
    heads, trees, kv_heads, group, resp,
    len_ref, guest_ref, adv_ref, partner_ref,
    q_hbm, k_hbm, v_hbm, up_hbm,
    gq_hbm, gk_hbm, gv_hbm,
    qv, cot, kx, vx, bias, weight, seen_scores, seen_top, gqv, pg, pf, rg, hg, hr, acc, fin, fout, gkv, gvv,
    there, there_mid, there_pick, there_out, far, back, back_mid, back_pick, back_out,
    loc, cloc, csend, crecv, hsend, hrecv, psend, precv, fsend, frecv,
    pgsend, pgrecv, hgsend, hgrecv, finsend, finrecv, oq, okv, there_sems, back_sems,
):
    h = lax.axis_index("head")
    s = lax.axis_index("seq")
    rows = q_hbm.shape[0]
    tiles = rows // TILE
    local_kv = kv_heads // heads
    width = group * HEAD_DIM
    half = kv_heads // 2
    pieces = 2 * half
    stride = trees // pieces
    core = lax.rem(h, 2)
    mate = h + 1 - 2 * core
    need = max((rows * b - PROMPT) % RESP_LEN for b in range(1, heads))
    need = -(-need // 16) * 16
    scaling = HEAD_DIM ** (-0.5)

    def send(src, dst, ssem, rsem, **where):
        return pltpu.make_async_remote_copy(
            src_ref=src, dst_ref=dst, send_sem=ssem, recv_sem=rsem, device_id=where, device_id_type=LOGICAL
        )

    def local(src, dst, sem):
        return pltpu.make_async_copy(src, dst, sem)

    own_copies = [
        local(k_hbm, kx.at[pl.ds(PAD + HALO, rows)], loc.at[0]),
        local(v_hbm, vx.at[pl.ds(PAD + HALO, rows)], loc.at[1]),
        local(q_hbm, qv, loc.at[2]),
    ]
    own_prompt = [
        local(k_hbm.at[pl.ds(0, PROMPT)], kx.at[pl.ds(0, PROMPT)], loc.at[3]),
        local(v_hbm.at[pl.ds(0, PROMPT)], vx.at[pl.ds(0, PROMPT)], loc.at[4]),
    ]
    own_cot = [
        local(
            up_hbm.at[pl.ds(pl.multiple_of(h * rows, TILE), rows), pl.ds(i * width, width)],
            cot.at[h * local_kv + i],
            cloc.at[i],
        )
        for i in range(local_kv)
    ]

    barrier = pltpu.get_barrier_semaphore()
    for m in range(1, heads):
        pl.semaphore_signal(barrier, inc=1, device_id={"head": mix(h, m, heads)}, device_id_type=LOGICAL)

    @pl.loop(1, trees)
    def _(d):
        pl.semaphore_signal(barrier, inc=1, device_id={"seq": lax.rem(s + d, trees)}, device_id_type=LOGICAL)

    @pl.when(h == 0)
    def _():
        for c in own_prompt:
            c.start()

    for c in own_copies + own_cot:
        c.start()
    pl.semaphore_wait(barrier, heads + trees - 2)

    def prompt_copy(a, to):
        src, dst = ((k_hbm, kx), (v_hbm, vx))[a]
        return send(
            src.at[pl.ds(0, PROMPT)], dst.at[pl.ds(0, PROMPT)], psend.at[a, to], precv.at[a], head=to
        )

    def halo_copy(a, to):
        src, dst = ((k_hbm, kx), (v_hbm, vx))[a]
        return send(
            src.at[pl.ds(rows - need, need)], dst.at[pl.ds(PAD + HALO - need, need)], hsend.at[a], hrecv.at[a],
            head=to,
        )

    def cot_copy(m, i):
        p = mix(h, m, heads)
        return send(
            up_hbm.at[pl.ds(pl.multiple_of(p * rows, TILE), rows), pl.ds(i * width, width)],
            cot.at[h * local_kv + i],
            csend.at[m * local_kv + i],
            crecv.at[h * local_kv + i],
            head=p,
        )

    def pass_on(a):
        dst = (kx, vx)[a].at[pl.ds(0, PROMPT)]
        return send(dst, dst, psend.at[a, 0], precv.at[a], head=h + 1)

    first_hop = [1] + list(range(2, heads, 2))

    @pl.when(h == 0)
    def _():
        for to in reversed(first_hop):
            for a in range(2):
                prompt_copy(a, to).start()

    @pl.when(h < heads - 1)
    def _():
        for a in range(2):
            halo_copy(a, h + 1).start()

    n_far = (heads - 2) * local_kv

    def far_chunk(n):
        return cot_copy(2 + lax.div(n, local_kv), lax.rem(n, local_kv))

    for i in range(local_kv):
        cot_copy(1, i).start()
    for n in range(min(2, n_far)):
        far_chunk(jnp.int32(n)).start()

    zero_pad = jnp.zeros((PAD - 2 * PROMPT, kx.shape[1]), BF16)
    kx[pl.ds(2 * PROMPT, PAD - 2 * PROMPT), :] = zero_pad
    vx[pl.ds(2 * PROMPT, PAD - 2 * PROMPT), :] = zero_pad

    if need < HALO:
        zero_rest = jnp.zeros((HALO - need, kx.shape[1]), BF16)
        kx[pl.ds(PAD, HALO - need), :] = zero_rest
        vx[pl.ds(PAD, HALO - need), :] = zero_rest

    @pl.when(h == 0)
    def _():
        zero_halo = jnp.zeros((need, kx.shape[1]), BF16)
        kx[pl.ds(PAD + HALO - need, need), :] = zero_halo
        vx[pl.ds(PAD + HALO - need, need), :] = zero_halo
        for c in own_prompt:
            c.wait()

    @pl.when(h > 0)
    def _():
        for a in range(2):
            prompt_copy(a, h).wait_recv()

    @pl.when((h > 1) & (core == 0))
    def _():
        for a in range(2):
            pass_on(a).start()

    def to_middle(bufs, sems, q):
        out, mid, _, _ = bufs
        return send(out.at[q], mid.at[s], sems.at[0, q], sems.at[1, s], seq=q * stride)

    def from_middle(bufs, sems, d):
        _, _, pick, done = bufs
        q = lax.div(s, stride)
        return send(pick.at[d], done.at[q], sems.at[2, d], sems.at[3, q], seq=d)

    def start_exchange(bufs, sems):
        out, mid, _, _ = bufs
        for q in range(pieces):

            @pl.when(s != q * stride)
            def _():
                to_middle(bufs, sems, q).start()

            @pl.when(s == q * stride)
            def _():
                mid[s] = out[q]

    def turn_exchange(bufs, sems):
        out, mid, pick, done = bufs

        @pl.when(lax.rem(s, stride) == 0)
        def _():
            @pl.loop(1, trees)
            def _(d):
                t = lax.rem(s + d, trees)
                send(out.at[0], mid.at[t], sems.at[0, 0], sems.at[1, t], seq=t).wait_recv()

            @pl.loop(1, trees)
            def _(d):
                t = lax.rem(s + d, trees)
                pick[t] = mid[partner_ref[t]]
                from_middle(bufs, sems, t).start()

            done[lax.div(s, stride)] = mid[partner_ref[s]]

    def finish_exchange(bufs, sems):
        _, _, pick, done = bufs
        for q in range(pieces):

            @pl.when(s != q * stride)
            def _():
                send(pick.at[0], done.at[q], sems.at[2, 0], sems.at[3, q], seq=q * stride).wait_recv()

    def sent_exchange(bufs, sems):
        for q in range(pieces):

            @pl.when(s != q * stride)
            def _():
                to_middle(bufs, sems, q).wait_send()

        @pl.when(lax.rem(s, stride) == 0)
        def _():
            @pl.loop(1, trees)
            def _(d):
                from_middle(bufs, sems, lax.rem(s + d, trees)).wait_send()

    there_bufs = (there, there_mid, there_pick, there_out)
    back_bufs = (back, back_mid, back_pick, back_out)

    def lanes(side, i):
        return pl.ds(pl.multiple_of((side * half + i) * HEAD_DIM, HEAD_DIM), HEAD_DIM)

    for i in range(half):
        there[i] = kx[0:PROMPT, lanes(core, i)]
        there[half + i] = vx[0:PROMPT, lanes(core, i)]
    start_exchange(there_bufs, there_sems)

    row_w = lax.broadcasted_iota(jnp.int32, (rows, HEAD_DIM), 0) + h * rows
    w = jnp.ones((rows, HEAD_DIM), F32)
    for r in range(resp):
        begin = PROMPT + r * RESP_LEN
        inside = (row_w >= begin) & (row_w < begin + RESP_LEN)
        w = jnp.where(inside, jnp.where(row_w - begin < len_ref[0, r], adv_ref[0, r], 0.0), w)
    weight[...] = w
    for t in range(tiles):
        row = lax.broadcasted_iota(jnp.int32, (8, TILE), 1) + (h * rows + t * TILE)
        begin_of = jnp.full((8, TILE), 1 << 20, jnp.int32)
        guest = jnp.zeros((8, TILE), jnp.int32)
        for r in range(resp):
            begin = PROMPT + r * RESP_LEN
            inside = (row >= begin) & (row < begin + RESP_LEN)
            begin_of = jnp.where(inside, begin, begin_of)
            guest = jnp.where(inside, guest_ref[0, r], guest)
        row, begin_of, guest = row[0:1], begin_of[0:1], guest[0:1]
        col = lax.broadcasted_iota(jnp.int32, (PAD, TILE), 0)
        seen_own = (col < PROMPT) & (guest == 0) & (col <= row)
        seen_far = (col >= PROMPT) & (col < 2 * PROMPT) & (guest == 1)
        bias[t, 0:PAD, :] = jnp.where(seen_own | seen_far, 0.0, -1e30)
        key = lax.broadcasted_iota(jnp.int32, (2 * TILE, TILE), 0) + (h * rows + (t - 1) * TILE)
        bias[t, PAD:, :] = jnp.where((key >= begin_of) & (key <= row), 0.0, -1e30)

    for c in own_copies:
        c.wait()

    @pl.when(h > 0)
    def _():
        for a in range(2):
            halo_copy(a, h).wait_recv()

    def stacked(j, t):
        return jnp.concatenate(
            [
                qv[
                    t * TILE : (t + 1) * TILE,
                    pl.ds(pl.multiple_of(j * width + g * HEAD_DIM, HEAD_DIM), HEAD_DIM),
                ]
                for g in range(group)
            ],
            axis=0,
        )

    def score_rows(j):
        cols = pl.ds(pl.multiple_of(j * HEAD_DIM, HEAD_DIM), HEAD_DIM)
        for t in range(tiles):
            win = slice(PAD + t * TILE, PAD + (t + 2) * TILE)
            sc = dot(kx[win, cols], stacked(j, t), 1, 1)
            sc = sc + jnp.concatenate([bias[t, PAD:, :]] * group, axis=1)
            seen_scores[j, t] = sc
            seen_top[j, t] = jnp.max(sc, axis=0, keepdims=True)

    @pl.loop(0, kv_heads // 2)
    def _(j):
        score_rows(j)

    turn_exchange(there_bufs, there_sems)

    @pl.loop(kv_heads // 2, kv_heads)
    def _(j):
        score_rows(j)

    finish_exchange(there_bufs, there_sems)

    def far_copy():
        return send(there_out, far, fsend.at[0], frecv.at[0], head=mate)

    far_copy().start()
    low = slice(PROMPT, 2 * PROMPT)
    for i in range(half):
        kx[low, lanes(core, i)] = there_out[i]
        vx[low, lanes(core, i)] = there_out[half + i]
    far_copy().wait_recv()
    for i in range(half):
        kx[low, lanes(1 - core, i)] = far[i]
        vx[low, lanes(1 - core, i)] = far[half + i]

    def part_copy(j, src, o):
        return send(
            pg.at[j], rg.at[src, lax.rem(j, half)], pgsend.at[j], pgrecv.at[src, lax.rem(j, half)], head=o
        )

    def part_arrival(src, i):
        return send(pg.at[0], rg.at[src, i], pgsend.at[0], pgrecv.at[src, i], head=src)

    def strip_copy(j, to):
        return send(
            hg.at[j, pl.ds(HALO - need, need)], hr.at[j], hgsend.at[j], hgrecv.at[j], head=to
        )

    def out_copy(j):
        return local(gqv.at[j], gq_hbm.at[:, pl.ds(pl.multiple_of(j * width, width), width)], oq.at[j])

    @pl.loop(0, kv_heads)
    def _(n):
        m = lax.div(n, local_kv)
        i = lax.rem(n, local_kv)
        p = mix(h, m, heads)
        j = p * local_kv + i

        @pl.when(m == 0)
        def _():
            local(
                up_hbm.at[pl.ds(0, rows), pl.ds(0, width)], cot.at[j], cloc.at[i]
            ).wait()

        @pl.when(m > 0)
        def _():
            send(cot.at[j], cot.at[j], csend.at[j], crecv.at[j], head=p).wait_recv()

        cols = pl.ds(pl.multiple_of(j * HEAD_DIM, HEAD_DIM), HEAD_DIM)
        k_prompt, v_prompt = kx[0:PAD, cols], vx[0:PAD, cols]
        dk_parts = [None] * (tiles + 2)
        dv_parts = [None] * (tiles + 2)

        def add(parts, at, x):
            parts[at] = x if parts[at] is None else parts[at] + x

        for t in range(tiles):
            span = slice(t * TILE, (t + 1) * TILE)
            win = slice(PAD + t * TILE, PAD + (t + 2) * TILE)
            k_win = jnp.concatenate([k_prompt, kx[win, cols]], axis=0)
            v_win = jnp.concatenate([v_prompt, vx[win, cols]], axis=0)
            q4 = stacked(j, t)
            wt = weight[span, :]
            c4 = jnp.concatenate(
                [
                    (cot[j, span, g * HEAD_DIM : (g + 1) * HEAD_DIM].astype(F32) * wt).astype(BF16)
                    for g in range(group)
                ],
                axis=0,
            )
            first = dot(k_prompt, q4, 1, 1) + jnp.concatenate([bias[t, 0:PAD, :]] * group, axis=1)
            top = jnp.maximum(jnp.max(first, axis=0, keepdims=True), seen_top[j, t])
            sc = jnp.concatenate([first, seen_scores[j, t]], axis=0)
            e = jnp.exp2((sc - top) * (scaling * math.log2(math.e)))
            prob = e * (1.0 / jnp.sum(e, axis=0, keepdims=True))
            gp = dot(v_win, c4, 1, 1)
            inner = jnp.sum(prob * gp, axis=0, keepdims=True)
            ds_low = (prob * (gp - inner)).astype(BF16)
            dv = dot(prob.astype(BF16), c4, 1, 0)
            dk = dot(ds_low, q4, 1, 0)
            dq = (dot(k_win, ds_low, 0, 0) * scaling).astype(BF16).T
            for g in range(group):
                gqv[j, span, g * HEAD_DIM : (g + 1) * HEAD_DIM] = dq[g * TILE : (g + 1) * TILE]
            add(dk_parts, 0, dk[0:PAD])
            add(dv_parts, 0, dv[0:PAD])
            for u in range(2):
                add(dk_parts, 1 + t + u, dk[PAD + u * TILE : PAD + (u + 1) * TILE])
                add(dv_parts, 1 + t + u, dv[PAD + u * TILE : PAD + (u + 1) * TILE])
        out_copy(j).start()
        both = [
            jnp.concatenate([a * scaling, b], axis=1) for a, b in zip(dk_parts, dv_parts)
        ]

        owner = lax.div(j, half)

        @pl.when(h == owner)
        def _():
            pf[lax.rem(j, half)] = both[0][0 : 2 * PROMPT]

        @pl.when(h != owner)
        def _():
            pg[j] = both[0][0 : 2 * PROMPT].astype(BF16)
            part_copy(j, h, owner).start()

        @pl.when(h > 0)
        def _():
            hg[j] = both[1].astype(BF16)
            strip_copy(j, h - 1).start()

        for t in range(tiles):
            acc[j, t * TILE : (t + 1) * TILE, :] = both[2 + t]

        @pl.when(n < n_far - 2)
        def _():
            far_chunk(n).wait_send()
            far_chunk(n + 2).start()

    @pl.when(h < 2)
    def _():
        for i in range(half):
            total = pf[i]
            for m in range(1, heads):
                part_arrival(mix(h, m, heads), i).wait_recv()
                total = total + rg[mix(h, m, heads), i].astype(F32)
            pf[i] = total
            back[i] = total[low, 0:HEAD_DIM].astype(BF16)
            back[half + i] = total[low, HEAD_DIM:].astype(BF16)
        start_exchange(back_bufs, back_sems)
        turn_exchange(back_bufs, back_sems)

    @pl.when(h < heads - 1)
    def _():
        for j in range(kv_heads):
            strip_copy(j, h).wait_recv()
            acc[j, rows - need : rows, :] = acc[j, rows - need : rows, :] + hr[j].astype(F32)

    for j in range(kv_heads):
        gkv[:, j * HEAD_DIM : (j + 1) * HEAD_DIM] = acc[j, :, 0:HEAD_DIM].astype(BF16)
        gvv[:, j * HEAD_DIM : (j + 1) * HEAD_DIM] = acc[j, :, HEAD_DIM:].astype(BF16)

    def rows_out(a, begin, count, at):
        src, dst = ((gkv, gk_hbm), (gvv, gv_hbm))[a]
        return local(src.at[pl.ds(begin, count)], dst.at[pl.ds(begin, count)], okv.at[at])

    last = [rows_out(a, PROMPT, rows - PROMPT, a) for a in range(2)]
    top_rows = [rows_out(a, 0, PROMPT, 2 + a) for a in range(2)]
    for c in last:
        c.start()

    def fin_copy():
        return send(fout, fin, finsend.at[0], finrecv.at[0], head=0)

    @pl.when(h < 2)
    def _():
        finish_exchange(back_bufs, back_sems)
        for i in range(half):
            fout[i] = (pf[i, 0:PROMPT, 0:HEAD_DIM] + back_out[i].astype(F32)).astype(BF16)
            fout[half + i] = (pf[i, 0:PROMPT, HEAD_DIM:] + back_out[half + i].astype(F32)).astype(BF16)

    @pl.when(h == 1)
    def _():
        fin_copy().start()

    @pl.when(h == 0)
    def _():
        for o in range(2):
            if o == 1:
                send(fout, fin, finsend.at[0], finrecv.at[0], head=1).wait_recv()
            piece = (fout, fin)[o]
            for i in range(half):
                at = (o * half + i) * HEAD_DIM
                gkv[0:PROMPT, at : at + HEAD_DIM] = piece[i]
                gvv[0:PROMPT, at : at + HEAD_DIM] = piece[half + i]

    for c in top_rows:
        c.start()

    @pl.when(h == 0)
    def _():
        for to in first_hop:
            for a in range(2):
                prompt_copy(a, to).wait_send()

    @pl.when((h > 1) & (core == 0))
    def _():
        for a in range(2):
            pass_on(a).wait_send()

    @pl.when(h < heads - 1)
    def _():
        for a in range(2):
            halo_copy(a, h + 1).wait_send()

    for i in range(local_kv):
        cot_copy(1, i).wait_send()
    for n in range(max(0, n_far - 2), n_far):
        far_chunk(jnp.int32(n)).wait_send()
    far_copy().wait_send()
    sent_exchange(there_bufs, there_sems)
    for j in range(kv_heads):
        o = j // half

        @pl.when(h != o)
        def _():
            part_copy(jnp.int32(j), h, o).wait_send()

    @pl.when(h < 2)
    def _():
        sent_exchange(back_bufs, back_sems)

    @pl.when(h > 0)
    def _():
        for j in range(kv_heads):
            strip_copy(j, h - 1).wait_send()

    @pl.when(h == 1)
    def _():
        fin_copy().wait_send()

    for j in range(kv_heads):
        out_copy(j).wait()
    for c in last + top_rows:
        c.wait()


def hand_over(gq, gk, gv, gq_out, gk_out, gv_out, gq_mid, gk_mid, gv_mid, sems):
    ins, outs = [], []
    for src, mid, dst, parts in ((gq, gq_mid, gq_out, 8), (gk, gk_mid, gk_out, 2), (gv, gv_mid, gv_out, 2)):
        size = src.shape[0] // parts
        for i in range(parts):
            at = pl.ds(i * size, size)
            ins.append(pltpu.make_async_copy(src.at[at], mid.at[at], sems.at[0, len(ins)]))
            outs.append(pltpu.make_async_copy(mid.at[at], dst.at[at], sems.at[1, len(outs)]))
    for c in ins:
        c.start()
    for c, d in zip(ins, outs):
        c.wait()
        d.start()
    for d in outs:
        d.wait()


def solution(mesh):
    heads, trees = mesh.shape["head"], mesh.shape["seq"]

    def step(queries, keys, values, upstream, lengths, guests, advantage, partner):
        rows, q_width = queries.shape
        kv_width = keys.shape[1]
        kv_heads = kv_width // HEAD_DIM
        group = q_width // kv_width
        local_kv = kv_heads // heads
        half = kv_heads // 2
        need = max((rows * b - PROMPT) % RESP_LEN for b in range(1, heads))
        need = -(-need // 16) * 16
        width = group * HEAD_DIM
        ext = PAD + HALO + rows
        tiles = rows // TILE
        win = PAD + 2 * TILE
        dma = pltpu.SemaphoreType.DMA
        scratch = [
            pltpu.VMEM((rows, q_width), BF16),
            pltpu.VMEM((kv_heads, rows, width), BF16),
            pltpu.VMEM((ext, kv_width), BF16),
            pltpu.VMEM((ext, kv_width), BF16),
            pltpu.VMEM((tiles, win, TILE), F32),
            pltpu.VMEM((rows, HEAD_DIM), F32),
            pltpu.VMEM((kv_heads, tiles, 2 * TILE, group * TILE), F32),
            pltpu.VMEM((kv_heads, tiles, 1, group * TILE), F32),
            pltpu.VMEM((kv_heads, rows, width), BF16),
            pltpu.VMEM((kv_heads, 2 * PROMPT, 256), BF16),
            pltpu.VMEM((half, 2 * PROMPT, 256), F32),
            pltpu.VMEM((heads, half, 2 * PROMPT, 256), BF16),
            pltpu.VMEM((kv_heads, HALO, 256), BF16),
            pltpu.VMEM((kv_heads, need, 256), BF16),
            pltpu.VMEM((kv_heads, rows, 256), F32),
            pltpu.VMEM((2 * half, PROMPT, HEAD_DIM), BF16),
            pltpu.VMEM((2 * half, PROMPT, HEAD_DIM), BF16),
            pltpu.VMEM((rows, kv_width), BF16),
            pltpu.VMEM((rows, kv_width), BF16),
            *[pltpu.VMEM((n, PROMPT, HEAD_DIM), BF16) for n in (2 * half, trees, trees, 2 * half, 2 * half)],
            *[pltpu.VMEM((n, PROMPT, HEAD_DIM), BF16) for n in (2 * half, trees, trees, 2 * half)],
            dma((5,)), dma((local_kv,)), dma((kv_heads,)), dma((kv_heads,)),
            dma((2,)), dma((2,)), dma((2, heads)), dma((2,)), dma((1,)), dma((1,)),
            dma((kv_heads,)), dma((heads, half)), dma((kv_heads,)), dma((kv_heads,)),
            dma((1,)), dma((1,)), dma((kv_heads,)), dma((4,)),
            dma((4, max(trees, 2 * half))), dma((4, max(trees, 2 * half))),
        ]
        smem = pl.BlockSpec(memory_space=pltpu.SMEM)
        anywhere = pl.BlockSpec(memory_space=pl.ANY)
        grads = pl.pallas_call(
            functools.partial(kernel, heads, trees, kv_heads, group, lengths.shape[1]),
            out_shape=(
                jax.ShapeDtypeStruct(queries.shape, BF16),
                jax.ShapeDtypeStruct(keys.shape, BF16),
                jax.ShapeDtypeStruct(values.shape, BF16),
            ),
            in_specs=[smem] * 4 + [anywhere] * 4,
            out_specs=(anywhere,) * 3,
            scratch_shapes=scratch,
            compiler_params=pltpu.CompilerParams(
                collective_id=0, has_side_effects=True, vmem_limit_bytes=56 * 1024 * 1024
            ),
        )(lengths, guests, advantage, partner, queries, keys, values, upstream)
        return pl.pallas_call(
            hand_over,
            out_shape=tuple(jax.ShapeDtypeStruct(x.shape, x.dtype) for x in grads),
            in_specs=[anywhere] * 3,
            out_specs=(anywhere,) * 3,
            scratch_shapes=[*[pltpu.VMEM(x.shape, x.dtype) for x in grads], dma((2, 12))],
        )(*grads)

    return jax.shard_map(
        step,
        mesh=mesh,
        in_specs=(
            P(("seq", "head"), None),
            P(("seq", "head"), None),
            P(("seq", "head"), None),
            P("seq", "head"),
            P("seq", None),
            P("seq", None),
            P("seq", None),
            P(),
        ),
        out_specs=(P(("seq", "head"), None), P(("seq", "head"), None), P(("seq", "head"), None)),
        check_vma=False,
    )
```

profile of v0, /device:TPU:0, one launch (start us, length us, event | category | flops | bytes accessed | tf_op | source)
XLA Modules:
  0.0 65.6 jit_solution(1434138039671611902)
XLA Ops:
  0.6 62.2 %shard_map.103 = (bf16[256,4096]{1,0:T(8,128)(2,1)}, bf16[256,1024]{1,0:T(8,128)(2,1)}, bf16[256,1024]{1,0:T(8,128)(2,1)}) custom-call(s32[1,8]{1,0:T(1,128)} %len_ref.1, s32[1,8]{1,0:T(1,128)} %guest_ref.1, f32[1,8]{1,0:T(1,128)} %adv_ref.1, s32[8]{0:T(128)} %partner_ref.1, bf16[256,4096]{1,0:T(8,128)(2,1)} %q_hbm.1, bf16[256,1024]{1,0:T(8,128)(2,1)} %k_hbm.1, ...), custom_call_target="tpu_custom_call" | custom-call | tf_op jit(solution)/shard_map/pallas_call | solution.py:603
  62.8 2.8 %shard_map.104 = (bf16[256,4096]{1,0:T(8,128)(2,1)}, bf16[256,1024]{1,0:T(8,128)(2,1)}, bf16[256,1024]{1,0:T(8,128)(2,1)}) custom-call(bf16[256,4096]{1,0:T(8,128)(2,1)} %get-tuple-element.6.gq, bf16[256,1024]{1,0:T(8,128)(2,1)} %get-tuple-element.7.gk, bf16[256,1024]{1,0:T(8,128)(2,1)} %get-tuple-element.8.gv), custom_call_target="tpu_custom_call" | custom-call | tf_op jit(solution)/shard_map/pallas_call | solution.py:617
where the time goes:
time: 65.8 us; the launch traced here: 65.6 us
  Pallas kernels  65 us (99%)
    pallas_call x1, Pallas kernels, step(): pl.pallas_call(functools.partial(kernel, heads, trees, kv_heads, group, l...  62.2 us
    pallas_call x1, Pallas kernels, step(): pl.pallas_call(hand_over, out_shape=tuple((jax.ShapeDtypeStruct(x.shape,...  2.81 us

commit v1 on v0

--- a/solution.py
+++ b/solution.py
@@ -52,6 +52,8 @@
     pieces = 2 * half
     stride = trees // pieces
     core = lax.rem(h, 2)
+    upper = heads // 2
+    sums_here = (h == 0) | (h == upper)
     mate = h + 1 - 2 * core
     need = max((rows * b - PROMPT) % RESP_LEN for b in range(1, heads))
     need = -(-need // 16) * 16
@@ -404,7 +406,7 @@
             jnp.concatenate([a * scaling, b], axis=1) for a, b in zip(dk_parts, dv_parts)
         ]
 
-        owner = lax.div(j, half)
+        owner = (1 - lax.div(j, half)) * upper
 
         @pl.when(h == owner)
         def _():
@@ -428,7 +430,7 @@
             far_chunk(n).wait_send()
             far_chunk(n + 2).start()
 
-    @pl.when(h < 2)
+    @pl.when(sums_here)
     def _():
         for i in range(half):
             total = pf[i]
@@ -463,23 +465,23 @@
     def fin_copy():
         return send(fout, fin, finsend.at[0], finrecv.at[0], head=0)
 
-    @pl.when(h < 2)
+    @pl.when(sums_here)
     def _():
         finish_exchange(back_bufs, back_sems)
         for i in range(half):
             fout[i] = (pf[i, 0:PROMPT, 0:HEAD_DIM] + back_out[i].astype(F32)).astype(BF16)
             fout[half + i] = (pf[i, 0:PROMPT, HEAD_DIM:] + back_out[half + i].astype(F32)).astype(BF16)
 
-    @pl.when(h == 1)
+    @pl.when(h == upper)
     def _():
         fin_copy().start()
 
     @pl.when(h == 0)
     def _():
-        for o in range(2):
-            if o == 1:
-                send(fout, fin, finsend.at[0], finrecv.at[0], head=1).wait_recv()
-            piece = (fout, fin)[o]
+        for o in (1, 0):
+            if o == 0:
+                send(fout, fin, finsend.at[0], finrecv.at[0], head=upper).wait_recv()
+            piece = (fin, fout)[o]
             for i in range(half):
                 at = (o * half + i) * HEAD_DIM
                 gkv[0:PROMPT, at : at + HEAD_DIM] = piece[i]
@@ -511,13 +513,13 @@
     far_copy().wait_send()
     sent_exchange(there_bufs, there_sems)
     for j in range(kv_heads):
-        o = j // half
+        o = (1 - j // half) * upper
 
         @pl.when(h != o)
         def _():
             part_copy(jnp.int32(j), h, o).wait_send()
 
-    @pl.when(h < 2)
+    @pl.when(sums_here)
     def _():
         sent_exchange(back_bufs, back_sems)
 
@@ -526,7 +528,7 @@
         for j in range(kv_heads):
             strip_copy(j, h - 1).wait_send()
 
-    @pl.when(h == 1)
+    @pl.when(h == upper)
     def _():
         fin_copy().wait_send()
 

time: 65.8 us -> 61 us (0.927)
  Pallas kernels: 65 us -> 60.2 us
    pallas_call x1, Pallas kernels: 62.2 us -> 57.3 us  [step(): pl.pallas_call(functools.partial(kernel, heads, trees, kv_heads, group, l...]
where the time goes in v1:
time: 61 us; the launch traced here: 60.8 us
  Pallas kernels  60.2 us (99%)
  between operations  0.64 us (1%)
    pallas_call x1, Pallas kernels, step(): pl.pallas_call(functools.partial(kernel, heads, trees, kv_heads, group, l...  57.3 us
    pallas_call x1, Pallas kernels, step(): pl.pallas_call(hand_over, out_shape=tuple((jax.ShapeDtypeStruct(x.shape,...  2.81 us

profile of v1, /device:TPU:0, one launch (start us, length us, event | category | flops | bytes accessed | tf_op | source)
XLA Modules:
  0.0 60.8 jit_solution(5290184350265442968)
XLA Ops:
  0.6 57.3 %shard_map.103 = (bf16[256,4096]{1,0:T(8,128)(2,1)}, bf16[256,1024]{1,0:T(8,128)(2,1)}, bf16[256,1024]{1,0:T(8,128)(2,1)}) custom-call(s32[1,8]{1,0:T(1,128)} %len_ref.1, s32[1,8]{1,0:T(1,128)} %guest_ref.1, f32[1,8]{1,0:T(1,128)} %adv_ref.1, s32[8]{0:T(128)} %partner_ref.1, bf16[256,4096]{1,0:T(8,128)(2,1)} %q_hbm.1, bf16[256,1024]{1,0:T(8,128)(2,1)} %k_hbm.1, ...), custom_call_target="tpu_custom_call" | custom-call | tf_op jit(solution)/shard_map/pallas_call | solution.py:605
  58.0 2.8 %shard_map.104 = (bf16[256,4096]{1,0:T(8,128)(2,1)}, bf16[256,1024]{1,0:T(8,128)(2,1)}, bf16[256,1024]{1,0:T(8,128)(2,1)}) custom-call(bf16[256,4096]{1,0:T(8,128)(2,1)} %get-tuple-element.6.gq, bf16[256,1024]{1,0:T(8,128)(2,1)} %get-tuple-element.7.gk, bf16[256,1024]{1,0:T(8,128)(2,1)} %get-tuple-element.8.gv), custom_call_target="tpu_custom_call" | custom-call | tf_op jit(solution)/shard_map/pallas_call | solution.py:619
